TPU v7x, 256 devices: a whole 4x4x8 slice. The times are simulated.
256 devices in a mesh: role: 2 (over core), grp: 8 (over z), dp: 16 (over y, x).
Axes of the slice: x: 4, y: 4, z: 8, core: 2. Of those that a mesh axis runs over, the one named last changes fastest.
Arguments:
- attn_parts: bfloat16 [8, 1536, 7168], P('grp', 'role', 'dp'), may hold values from -3 to 3
- residual: bfloat16 [1536, 7168], P(('role', 'grp', 'dp')), may hold values from -6 to 6
- norm_gain: bfloat16 [7168], replicated, may hold values from 0.099609375 to 1.8984375
- router_weight: bfloat16 [7168, 32], replicated, may hold values from -0.0625 to 0.0625
- expert_ids: int32 [1536, 8], P(('role', 'grp', 'dp')), may hold values from 0 to 31, all different within a row; in each aligned block of 6 rows (0 to 5, 6 to 11, ...) at most 2 rows name the same one
- w_gate: bfloat16 [32, 7168, 2048], P(('role', 'dp'), None, 'grp'), may hold values from -0.0625 to 0.0625
- w_up: bfloat16 [32, 7168, 2048], P(('role', 'dp'), None, 'grp'), may hold values from -0.0625 to 0.0625
- w_down: bfloat16 [32, 2048, 7168], P(('role', 'dp'), 'grp'), may hold values from -0.125 to 0.125
Outputs:
- mixed: bfloat16 [1536, 7168], P(('role', 'grp', 'dp'))
Inputs may be any that keep to these rules, and one draw needn't show every extreme that they name: `expert_ids`: each row names 8 different experts. Among the 6 rows of one device no expert is named by more than 2 rows, and in every draw the rows of some device name some expert exactly 2 times.
All inputs are finite; a program needn't handle non-finite values.
Results may differ from a plain program's by a relative error of at most 0.012.
Values may be sent and summed in bfloat16 or wider, within the bound.
No kernel may reach another device: no remote copies, remote signals or barrier semaphores. Data moves between devices by JAX's collectives and lax.ppermute only.
A program may use at most 128 MiB of HBM per device.

v0:
```python
import jax
import jax.numpy as jnp
from jax import lax
from jax.sharding import PartitionSpec as P

CAP = 2


norm_eps = 1e-06
route_scale = 2.5


def local(attn_parts, residual, norm_gain, router_weight, expert_ids, w_gate, w_up, w_down):
    grp_count = lax.axis_size("grp")
    dp_count = lax.axis_size("dp")
    groups = lax.axis_size("role") * dp_count
    own_part = attn_parts[0]
    rows_dev = residual.shape[0]
    model_width = residual.shape[1]
    col_width = own_part.shape[1]
    pieces = own_part.reshape(grp_count * dp_count, rows_dev, col_width)
    received = lax.all_to_all(pieces, ("grp", "dp"), split_axis=0, concat_axis=2, tiled=True)
    received = received.reshape(rows_dev, grp_count, dp_count * col_width)
    attention = jnp.sum(received.astype(jnp.float32), axis=1)
    hidden = (residual.astype(jnp.float32) + attention).astype(jnp.bfloat16)
    hidden_f = hidden.astype(jnp.float32)
    meansq = jnp.mean(hidden_f * hidden_f, axis=-1, keepdims=True)
    normed = (hidden_f * lax.rsqrt(meansq + norm_eps) * norm_gain.astype(jnp.float32)).astype(
        jnp.bfloat16
    )
    scores = jax.nn.sigmoid(jnp.dot(normed, router_weight, preferred_element_type=jnp.float32))
    experts = router_weight.shape[1]
    local_experts = w_gate.shape[0]
    onehot = (expert_ids[:, :, None] == jnp.arange(experts, dtype=jnp.int32)).astype(jnp.float32)
    picked = jnp.sum(onehot * scores[:, None, :], axis=-1)
    weights = route_scale * picked / jnp.sum(picked, axis=-1, keepdims=True)
    per_expert = jnp.sum(onehot * weights[:, :, None], axis=1)
    chosen = jnp.sum(onehot, axis=1)
    slot_rank = jnp.cumsum(chosen, axis=0) - chosen
    slot_index = jnp.arange(CAP, dtype=jnp.int32).astype(jnp.float32)
    select = chosen[:, :, None] * (slot_rank[:, :, None] == slot_index).astype(jnp.float32)
    select_grouped = select.reshape(rows_dev, groups, local_experts, CAP)
    outbound = jnp.einsum(
        "jqec,jd->eqcd",
        select_grouped.astype(jnp.bfloat16),
        normed,
        preferred_element_type=jnp.float32,
    ).astype(jnp.bfloat16)
    arrived = lax.all_to_all(outbound, ("role", "dp"), split_axis=1, concat_axis=1, tiled=True)
    arrived = arrived.reshape(local_experts, groups * CAP, model_width)
    gathered_rows = lax.all_gather(arrived, "grp", axis=1, tiled=True)
    gate_val = jnp.einsum("esd,edf->esf", gathered_rows, w_gate, preferred_element_type=jnp.float32)
    up_val = jnp.einsum("esd,edf->esf", gathered_rows, w_up, preferred_element_type=jnp.float32)
    activated = (jax.nn.silu(gate_val) * up_val).astype(jnp.bfloat16)
    summed = lax.psum_scatter(
        jnp.einsum("esf,efd->sed", activated, w_down, preferred_element_type=jnp.float32).astype(
            jnp.bfloat16
        ),
        "grp",
        scatter_dimension=0,
        tiled=True,
    )
    results = summed.reshape(groups, CAP, local_experts, model_width)
    returned = lax.all_to_all(results, ("role", "dp"), split_axis=0, concat_axis=0, tiled=True)
    combine_mat = (select * per_expert[:, :, None]).reshape(rows_dev, groups, local_experts, CAP)
    routed = jnp.einsum("jqec,qced->jd", combine_mat, returned.astype(jnp.float32))
    return (hidden_f + routed).astype(jnp.bfloat16)


def solution(mesh):
    in_specs = (
        P("grp", "role", "dp"),
        P(("role", "grp", "dp"), None),
        P(),
        P(),
        P(("role", "grp", "dp"), None),
        P(("role", "dp"), None, "grp"),
        P(("role", "dp"), None, "grp"),
        P(("role", "dp"), "grp", None),
    )
    out_specs = P(("role", "grp", "dp"), None)
    return jax.shard_map(local, mesh=mesh, in_specs=in_specs, out_specs=out_specs, check_vma=False)
```

profile of v0, /device:TPU:1, one launch (start us, length us, event | category | flops | bytes accessed | tf_op | source)
XLA Modules:
  0.0 300.3 jit_solution(18253186181973739135)
XLA Ops:
  6.5 0.0 copy-start
  6.5 0.0 copy-start.2
  6.5 1.4 copy.19
  8.0 1.3 reshape_squeeze.3
  9.3 16.3 %all-to-all-start = ((bf16[128,6,448]{2,1,0:T(8,128)(2,1)}), bf16[128,6,448]{2,1,0:T(8,128)(2,1)S(1)}, u32[]{:S(2)}, u32[]{:S(2)}) async-start(bf16[128,6,448]{2,1,0:T(8,128)(2,1)} %reshape_squeeze.3), calls=%async_computation | async-start | bytes 2097152 | tf_op jit(solution)/shard_map/all_to_all | solution.py:22
  25.6 0.0 all-gather.2.cloned.1.call-start
  25.7 0.0 copy-done.2
  25.7 0.5 iota_convert_fusion
  26.2 28.0 %all-to-all-done = bf16[128,6,448]{2,1,0:T(8,128)(2,1)S(1)} async-done(((bf16[128,6,448]{2,1,0:T(8,128)(2,1)}), bf16[128,6,448]{2,1,0:T(8,128)(2,1)S(1)}, u32[]{:S(2)}, u32[]{:S(2)}) %all-to-all-start) | async-done | bytes 688160 | tf_op jit(solution)/shard_map/all_to_all | solution.py:22
  54.2 0.3 convert_bitcast_fusion
  54.5 0.9 copy.20
  55.5 0.0 copy-start.1
  55.5 0.7 reshape.100
  56.1 0.3 reduce_sum.54
  56.5 1.1 fusion.36
  57.5 0.0 copy-done
  57.6 0.3 fusion.23
  57.8 0.0 copy-done.1
  57.8 0.2 select_reduce_fusion
  58.1 0.1 multiply_divide_fusion
  58.1 0.1 select_reduce_fusion.2
  58.3 1.2 fusion.1
  59.4 0.9 copy.21
  60.4 21.9 %all_to_all.19 = bf16[1,32,2,7168]{3,2,0,1:T(2,128)(2,1)S(1)} all-to-all(bf16[1,32,2,7168]{3,2,0,1:T(2,128)(2,1)S(1)} %copy.21), channel_id=1, replica_groups=mesh['role'=2,'grp'=8,'dp'=16] {'role','dp'}, dimensions={1} | all-to-all | bytes 1835008 | tf_op jit(solution)/shard_map/all_to_all | solution.py:49
  82.2 1.3 reshape.93
  83.5 0.0 all-gather.2.cloned.1.call-update
  83.5 0.2 reduce-scatter.2.cloned.1.call-start
  83.8 77.9 %all-gather.2.cloned.1.call-done = bf16[1,512,7168]{2,1,0:T(8,128)(2,1)} async-done(((bf16[1,64,7168]{2,1,0:T(8,128)(2,1)}), bf16[1,512,7168]{2,1,0:T(8,128)(2,1)}) %all-gather.2.cloned.1.call-update) | async-done | bytes 7340048 | tf_op jit(solution)/shard_map/all_gather | solution.py:51
  161.6 6.2 %fusion.6 = f32[512,256]{1,0:T(8,128)S(1)} fusion(bf16[1,512,7168]{2,1,0:T(8,128)(2,1)} %all-gather.2.cloned.1.call-done, bf16[1,7168,256]{2,1,0:T(8,128)(2,1)} %param.13), kind=kOutput, calls=%fused_computation.9 | convolution fusion | flops 1879048192 | bytes 11534336 | tf_op jit(solution)/shard_map/esd,edf->esf/dot_general | solution.py:52
  167.8 16.0 %fusion = bf16[512,1,7168]{2,0,1:T(8,128)(2,1)} fusion(bf16[1,256,7168]{2,1,0:T(8,128)(2,1)} %param.15, bf16[1,7168,256]{2,1,0:T(8,128)(2,1)} %param.14, bf16[1,512,7168]{2,1,0:T(8,128)(2,1)} %all-gather.2.cloned.1.call-done, f32[512,256]{1,0:T(8,128)S(1)} %fusion.6), kind=kOutput, calls=%fused_computation.1 | convolution fusion | flops 3762552832 | bytes 22544384 | tf_op jit(solution)/shard_map/esf,efd->sed/dot_general | solution.py:56
  183.8 0.0 reduce-scatter.2.cloned.1.call-update
  183.8 0.0 copy-start.3
  183.9 83.8 %reduce-scatter.2.cloned.1.call-done = bf16[64,1,7168]{2,0,1:T(8,128)(2,1)} async-done(((bf16[512,1,7168]{2,0,1:T(8,128)(2,1)}), bf16[64,1,7168]{2,0,1:T(8,128)(2,1)}) %reduce-scatter.2.cloned.1.call-update) | async-done | bytes 917520 | tf_op jit(solution)/shard_map/reduce_scatter | solution.py:55
  267.7 2.3 reshape.98
  270.0 22.5 %all_to_all.20 = bf16[32,2,1,7168]{3,1,2,0:T(2,128)(2,1)S(1)} all-to-all(bf16[32,2,1,7168]{3,1,2,0:T(2,128)(2,1)S(1)} %bitcast.61), channel_id=1, replica_groups=mesh['role'=2,'grp'=8,'dp'=16] {'role','dp'}, dimensions={0} | all-to-all | bytes 1835008 | tf_op jit(solution)/shard_map/all_to_all | solution.py:64
  292.5 0.0 copy-done.3
  292.5 1.0 fusion.3
  (4 shorter events, 0.0 us)
Async XLA Ops:
  6.5 51.0 %copy-start = (bf16[7168,32]{0,1:T(8,128)(2,1)S(1)}, bf16[7168,32]{0,1:T(8,128)(2,1)}, u32[]{:S(2)}) copy-start(bf16[7168,32]{0,1:T(8,128)(2,1)} %param.11) | copy-start | bytes 1376260
  6.5 19.2 %copy-start.2 = (bf16[7168]{0:T(1024)(128)(2,1)S(1)}, bf16[7168]{0:T(1024)(128)(2,1)}, u32[]{:S(2)}) copy-start(bf16[7168]{0:T(1024)(128)(2,1)} %param.10) | copy-start | bytes 43012
  9.3 44.9 %all-to-all-start = ((bf16[128,6,448]{2,1,0:T(8,128)(2,1)}), bf16[128,6,448]{2,1,0:T(8,128)(2,1)S(1)}, u32[]{:S(2)}, u32[]{:S(2)}) async-start(bf16[128,6,448]{2,1,0:T(8,128)(2,1)} %reshape_squeeze.3), calls=%async_computation | async-start | bytes 2097152 | tf_op jit(solution)/shard_map/all_to_all | solution.py:22
  25.6 136.0 %all-gather.2.cloned.1.call-start = ((), (), s32[]{:S(2)}) async-start(), calls=%async_computation.4 | async-start | bytes 8257536 | tf_op jit(solution)/shard_map/all_gather | solution.py:51
  55.5 2.4 copy-start.1
  83.5 184.1 %reduce-scatter.2.cloned.1.call-start = ((), (), s32[]{:S(2)}) async-start(), calls=%async_computation.5 | async-start | bytes 8257536 | tf_op jit(solution)/shard_map/reduce_scatter | solution.py:55
  183.8 108.6 %copy-start.3 = (f32[2]{0:T(128)S(1)}, f32[2]{0:T(128)}, u32[]{:S(2)}) copy-start(f32[2]{0:T(128)} %iota_convert_fusion) | copy-start | bytes 28
Sparse Core Ops, SparseCore 0:
  83.7 77.9 all-gather.1
  184.0 83.6 reduce-scatter.1
where the time goes:
time: 301 us; the launch traced here: 300 us
  waiting for transfers between devices  190 us (63%)
  blocking collectives  44.3 us (15%)
  matrix products  24.7 us (8%)
  starting transfers between devices  16.6 us (6%)
  between operations  13.5 us (4%)
  local copies, waits for them, and re-layouts  8.9 us (3%)
    reduce_scatter x1, waiting for transfers between devices, local(): lax.psum_scatter(jnp.einsum('esf,efd->sed', activated, w_down, preferred_...  83.8 us
    all_gather x1, waiting for transfers between devices, local(): gathered_rows = lax.all_gather(arrived, 'grp', axis=1, tiled=True)  77.9 us
    all_to_all x1, waiting for transfers between devices, local(): lax.all_to_all(pieces, ('grp', 'dp'), split_axis=0, concat_axis=2, tiled=...  28 us
    all_to_all x1, blocking collectives, local(): lax.all_to_all(results, ('role', 'dp'), split_axis=0, concat_axis=0, tile...  22.5 us
    all_to_all x1, blocking collectives, local(): lax.all_to_all(outbound, ('role', 'dp'), split_axis=1, concat_axis=1, til...  21.9 us
    all_to_all x1, starting transfers between devices, local(): lax.all_to_all(pieces, ('grp', 'dp'), split_axis=0, concat_axis=2, tiled=...  16.3 us
    dot_general x1, matrix products, local(): jnp.einsum('esf,efd->sed', activated, w_down, preferred_element_type=jnp....  16 us
    dot_general x1, matrix products, local(): jnp.einsum('esd,edf->esf', gathered_rows, w_gate, preferred_element_type=...  6.18 us
  transfers between devices with their start and end apart: 3, of which 3 were waited for; matrix products, arithmetic and copies ran while one was open for 0% of the time, Pallas kernels for 0%

commit v1 on v0

v1 whole, which is shorter than its diff:
```python
import functools

import jax
import jax.numpy as jnp
from jax import lax
from jax.experimental import pallas as pl
from jax.experimental.pallas import tpu as pltpu
from jax.sharding import PartitionSpec as P

CAP = 2
B_COLS = 2560
UP_CHUNK = 1024
DOWN_CHUNK = 1024
VMEM_MIB = 40
AUX = 128
NO_EXPERT = 99.0

norm_eps = 1e-06
route_scale = 2.5
f32 = jnp.float32
bf16 = jnp.bfloat16


def iota(shape, dim):
    return lax.broadcasted_iota(jnp.int32, shape, dim)


def dot(a, b, contract=((1,), (0,))):
    return lax.dot_general(a, b, (contract, ((), ())), preferred_element_type=f32)


def split3(x):
    hi = x.astype(bf16)
    rest = x - hi.astype(f32)
    mid = rest.astype(bf16)
    lo = (rest - mid.astype(f32)).astype(bf16)
    return hi, mid, lo


def params():
    return pltpu.CompilerParams(vmem_limit_bytes=VMEM_MIB * 1024 * 1024)


def slots_of(ids, weight_cols, rows, rows_block, experts, per_expert_cols):
    blocks = rows // rows_block
    lane = iota((rows, experts), 1).astype(f32)
    chosen = jnp.zeros((rows, experts), f32)
    per_expert = jnp.zeros((rows, experts), f32)
    for k in range(len(weight_cols)):
        match = (ids[:, k : k + 1] == lane).astype(f32)
        chosen = chosen + match
        per_expert = per_expert + match * weight_cols[k]
    r, c = iota((rows, rows), 0), iota((rows, rows), 1)
    before = ((r // rows_block == c // rows_block) & (c < r)).astype(f32).astype(bf16)
    rank = dot(before, chosen.astype(bf16))
    cols = experts * per_expert_cols
    spread = (iota((experts, cols), 1) // per_expert_cols == iota((experts, cols), 0)).astype(f32).astype(bf16)
    hi, mid, lo = split3(per_expert)
    chosen_x = dot(chosen.astype(bf16), spread)
    rank_x = dot(rank.astype(bf16), spread)
    weight_x = dot(hi, spread) + dot(mid, spread) + dot(lo, spread)
    col = iota((rows, cols), 1)
    own = (col // CAP) % blocks == iota((rows, cols), 0) // rows_block
    select = jnp.where(own & (rank_x == (col % CAP).astype(f32)), chosen_x, 0.0)
    return select, select * weight_x


def route_body(rows_dev, top, experts, ca, hidden_ref, gain_ref, router_ref, ids_ref, out_ref, payload_ref, comb_ref):
    h = hidden_ref[...].astype(f32)
    rows, width = h.shape
    meansq = jnp.sum(h * h, axis=-1, keepdims=True) * (1.0 / width)
    normed = (h * lax.rsqrt(meansq + norm_eps) * gain_ref[...].astype(f32)).astype(bf16)
    scores = jax.nn.sigmoid(dot(normed, router_ref[...], ((1,), (1,))))
    ids = ids_ref[...].astype(f32)
    lane = iota((rows, experts), 1).astype(f32)
    picked = [
        jnp.sum(jnp.where(ids[:, k : k + 1] == lane, scores, 0.0), axis=-1, keepdims=True) for k in range(top)
    ]
    total = functools.reduce(lambda a, b: a + b, picked)
    total = jnp.where(iota((rows, 1), 0) < rows_dev, total, 1.0)
    weights = [route_scale * p / total for p in picked]
    select, combine = slots_of(ids, weights, rows, rows, experts, CAP)
    hi, mid, _ = split3(combine)
    comb_ref[:rows, :] = hi.astype(f32)
    comb_ref[rows:, :] = mid.astype(f32)
    out_ref[...] = dot(select.astype(bf16), normed[:, :ca], ((0,), (0,))).astype(bf16)
    payload_ref[:, : width - ca] = normed[:, ca:]
    at = iota((rows, AUX), 1)
    aux = jnp.zeros((rows, AUX), f32)
    for k in range(top):
        aux = jnp.where(at == k, ids[:, k : k + 1], aux)
        for part, value in enumerate(split3(weights[k])):
            aux = jnp.where(at == (part + 1) * top + k, value.astype(f32), aux)
    payload_ref[:, width - ca :] = aux.astype(bf16)


def route(hidden, gain, router_t, ids, rows_dev, ca):
    rows, width = hidden.shape
    experts, top = router_t.shape[0], ids.shape[1]
    return pl.pallas_call(
        functools.partial(route_body, rows_dev, top, experts, ca),
        out_shape=(
            jax.ShapeDtypeStruct((experts * CAP, ca), bf16),
            jax.ShapeDtypeStruct((rows, width - ca + AUX), bf16),
            jax.ShapeDtypeStruct((2 * rows, experts * CAP), f32),
        ),
        compiler_params=params(),
        name="route",
    )(hidden, gain, router_t, ids)


def spread_body(top, experts, rows_block, rows_ref, out_ref, comb_ref):
    rows = rows_ref.shape[0]
    blocks = rows // rows_block
    cb = rows_ref.shape[1] - AUX
    aux = rows_ref[:, cb:].astype(f32)
    ids = aux[:, :top]
    weights = [
        aux[:, top + k : top + k + 1] + aux[:, 2 * top + k : 2 * top + k + 1] + aux[:, 3 * top + k : 3 * top + k + 1]
        for k in range(top)
    ]
    select, combine = slots_of(ids, weights, rows, rows_block, experts, blocks * CAP)
    hi, mid, _ = split3(combine)
    comb_ref[:rows, :] = hi
    comb_ref[rows:, :] = mid
    out_ref[...] = dot(select.astype(bf16), rows_ref[:, :cb], ((0,), (0,))).astype(bf16)


def spread_rows(rows_in, top, experts, rows_block):
    rows, width = rows_in.shape
    slots = experts * (rows // rows_block) * CAP
    return pl.pallas_call(
        functools.partial(spread_body, top, experts, rows_block),
        out_shape=(
            jax.ShapeDtypeStruct((slots, width - AUX), bf16),
            jax.ShapeDtypeStruct((2 * rows, slots), bf16),
        ),
        compiler_params=params(),
        name="spread_rows",
    )(rows_in)


def reorder(slots, blocks, groups, to_block_major):
    row, col = iota((slots, slots), 0), iota((slots, slots), 1)
    if to_block_major:
        outer, inner = groups, blocks
    else:
        outer, inner = blocks, groups
    first, second, slot = row // (outer * CAP), (row // CAP) % outer, row % CAP
    return (col == (second * inner + first) * CAP + slot).astype(f32).astype(bf16)


def chunks_of(start, stop, size):
    return [(at, min(size, stop - at)) for at in range(start, stop, size)]


def loads(pieces, sem):
    copies = [pltpu.make_async_copy(src, dst, sem.at[i]) for i, (src, dst) in enumerate(pieces)]
    for copy in copies:
        copy.start()
    return copies


def up_loads(pieces, base, x_hbm, wg_hbm, wu_hbm, x_buf, wg_buf, wu_buf):
    out = []
    for at, size in pieces:
        here, there = pl.ds(at - base, size), pl.ds(at, size)
        out.append((x_hbm.at[:, here], x_buf.at[:, here]))
        out.append((wg_hbm.at[0, there, :], wg_buf.at[here, :]))
        out.append((wu_hbm.at[0, there, :], wu_buf.at[here, :]))
    return out


def up_sums(pieces, base, copies, x_buf, wg_buf, wu_buf, acc):
    ff = wg_buf.shape[1]
    for i, (at, size) in enumerate(pieces):
        for copy in copies[3 * i : 3 * i + 3]:
            copy.wait()
        here = pl.ds(at - base, size)
        x = x_buf[:, here]
        gate, up = dot(x, wg_buf[here, :]), dot(x, wu_buf[here, :])
        if i == 0:
            acc[:, :ff] = gate
            acc[:, ff:] = up
        else:
            acc[:, :ff] += gate
            acc[:, ff:] += up


def up_first_body(blocks, groups, base, x_hbm, wg_hbm, wu_hbm, part_ref, x_buf, wg_buf, wu_buf, acc, sem):
    pieces = chunks_of(base, wg_hbm.shape[1], UP_CHUNK)
    copies = loads(up_loads(pieces, base, x_hbm, wg_hbm, wu_hbm, x_buf, wg_buf, wu_buf), sem)
    order = reorder(acc.shape[0], blocks, groups, True)
    up_sums(pieces, base, copies, x_buf, wg_buf, wu_buf, acc)
    hi, mid, lo = split3(acc[...])
    part_ref[...] = dot(order, hi) + dot(order, mid) + dot(order, lo)


def up_first(x, w_gate, w_up, blocks, groups):
    slots, width = x.shape
    _, total, ff = w_gate.shape
    copies = 3 * len(chunks_of(total - width, total, UP_CHUNK))
    return pl.pallas_call(
        functools.partial(up_first_body, blocks, groups, total - width),
        in_specs=[pl.BlockSpec(memory_space=pl.ANY)] + [pl.BlockSpec(memory_space=pltpu.HBM)] * 2,
        out_shape=jax.ShapeDtypeStruct((slots, 2 * ff), f32),
        scratch_shapes=[
            pltpu.VMEM((slots, width), bf16),
            pltpu.VMEM((width, ff), bf16),
            pltpu.VMEM((width, ff), bf16),
            pltpu.VMEM((slots, 2 * ff), f32),
            pltpu.SemaphoreType.DMA((copies,)),
        ],
        compiler_params=params(),
        cost_estimate=pl.CostEstimate(
            flops=4 * slots * width * ff, bytes_accessed=2 * width * (slots + 2 * ff), transcendentals=0
        ),
        name="up_first",
    )(x, w_gate, w_up)


def rest_body(blocks, groups, part_hbm, x_hbm, wg_hbm, wu_hbm, wd_hbm, y_hbm, act_ref, *scratch):
    part_buf, x_buf, wg_buf, wu_buf, wd_buf, y_buf, acc, sem, y_sem = scratch
    slots, width = x_hbm.shape
    ff = wg_hbm.shape[2]
    pieces = chunks_of(0, width, UP_CHUNK)
    downs = chunks_of(0, width, DOWN_CHUNK)
    wanted = up_loads(pieces, 0, x_hbm, wg_hbm, wu_hbm, x_buf, wg_buf, wu_buf)
    wanted.append((part_hbm, part_buf))
    wanted.append((wd_hbm.at[0, :, pl.ds(0, width)], wd_buf))
    copies = loads(wanted, sem)
    up_sums(pieces, 0, copies, x_buf, wg_buf, wu_buf, acc)
    copies[-2].wait()
    gate = acc[:, :ff] + part_buf[:, :ff]
    up = acc[:, ff:] + part_buf[:, ff:]
    act = (gate / (1.0 + jnp.exp(-gate)) * up).astype(bf16)
    act_ref[...] = act
    copies[-1].wait()
    out = []
    for i, (at, size) in enumerate(downs):
        here = pl.ds(at, size)
        y_buf[:, here] = dot(act_ref[...], wd_buf[:, here]).astype(bf16)
        copy = pltpu.make_async_copy(y_buf.at[:, here], y_hbm.at[:, here], y_sem.at[i])
        copy.start()
        out.append(copy)
    for copy in out:
        copy.wait()


def up_rest_down(part, x, w_gate, w_up, w_down, blocks, groups):
    slots, width = x.shape
    ff = w_gate.shape[2]
    copies = 3 * len(chunks_of(0, width, UP_CHUNK)) + 2
    return pl.pallas_call(
        functools.partial(rest_body, blocks, groups),
        in_specs=[pl.BlockSpec(memory_space=pl.ANY)] + [pl.BlockSpec(memory_space=pltpu.HBM)] * 4,
        out_specs=[pl.BlockSpec(memory_space=pltpu.HBM), pl.BlockSpec(memory_space=pltpu.VMEM)],
        out_shape=(pltpu.HBM((slots, width), bf16), jax.ShapeDtypeStruct((slots, ff), bf16)),
        scratch_shapes=[
            pltpu.VMEM((slots, 2 * ff), f32),
            pltpu.VMEM((slots, width), bf16),
            pltpu.VMEM((width, ff), bf16),
            pltpu.VMEM((width, ff), bf16),
            pltpu.VMEM((ff, width), bf16),
            pltpu.VMEM((slots, width), bf16),
            pltpu.VMEM((slots, 2 * ff), f32),
            pltpu.SemaphoreType.DMA((copies,)),
            pltpu.SemaphoreType.DMA((len(chunks_of(0, width, DOWN_CHUNK)),)),
        ],
        compiler_params=params(),
        cost_estimate=pl.CostEstimate(
            flops=6 * slots * width * ff, bytes_accessed=2 * width * (2 * slots + 3 * ff), transcendentals=slots * ff
        ),
        name="up_rest_down",
    )(part, x, w_gate, w_up, w_down)


def down_body(blocks, groups, act_ref, wd_hbm, out_ref, wd_buf, act_buf, sem):
    slots, width = out_ref.shape
    base = wd_hbm.shape[2] - width
    downs = chunks_of(0, width, DOWN_CHUNK)
    copies = loads([(wd_hbm.at[0, :, pl.ds(base + at, size)], wd_buf.at[:, pl.ds(at, size)]) for at, size in downs], sem)
    act_buf[...] = dot(reorder(slots, blocks, groups, False), act_ref[...]).astype(bf16)
    for copy, (at, size) in zip(copies, downs):
        copy.wait()
        out_ref[:, pl.ds(at, size)] = dot(act_buf[...], wd_buf[:, pl.ds(at, size)]).astype(bf16)


def down(act, w_down, width, blocks, groups):
    slots, ff = act.shape
    return pl.pallas_call(
        functools.partial(down_body, blocks, groups),
        in_specs=[pl.BlockSpec(memory_space=pltpu.VMEM), pl.BlockSpec(memory_space=pltpu.HBM)],
        out_shape=jax.ShapeDtypeStruct((slots, width), bf16),
        scratch_shapes=[
            pltpu.VMEM((ff, width), bf16),
            pltpu.VMEM((slots, ff), bf16),
            pltpu.SemaphoreType.DMA((len(chunks_of(0, width, DOWN_CHUNK)),)),
        ],
        compiler_params=params(),
        cost_estimate=pl.CostEstimate(
            flops=2 * slots * width * ff, bytes_accessed=2 * width * (slots + ff), transcendentals=0
        ),
        name="down",
    )(act, w_down)


def local(attn_parts, residual, norm_gain, router_weight, expert_ids, w_gate, w_up, w_down):
    blocks = lax.axis_size("grp")
    dp_count = lax.axis_size("dp")
    groups = lax.axis_size("role") * dp_count
    plane = ("role", "dp")
    rows_dev, width = residual.shape
    experts = router_weight.shape[1]
    top = expert_ids.shape[1]
    cb = B_COLS
    ca = width - cb
    rows_pad = 8

    part = attn_parts[0]
    col_width = part.shape[1]
    tiles = -(-col_width // 128)
    pieces = jnp.pad(part, ((0, 0), (0, tiles * 128 - col_width)))
    pieces = pieces.reshape(blocks * dp_count, rows_dev * tiles, 128)
    received = lax.all_to_all(pieces, ("grp", "dp"), split_axis=0, concat_axis=0, tiled=True)
    received = received.reshape(blocks, dp_count, rows_dev * tiles, 128)
    attention = jnp.sum(received.astype(f32), axis=0)
    attention = attention.reshape(dp_count, rows_dev, tiles * 128)[:, :, :col_width]
    attention = attention.transpose(1, 0, 2).reshape(rows_dev, width)
    hidden = (residual.astype(f32) + attention).astype(bf16)
    hidden = jnp.pad(hidden, ((0, rows_pad - rows_dev), (0, 0)))

    ids = jnp.pad(expert_ids, ((0, rows_pad - rows_dev), (0, 0)), constant_values=int(NO_EXPERT))
    out_a, payload, comb_a = route(hidden, norm_gain[None], router_weight.T, ids, rows_dev, ca)

    arrived = lax.all_to_all(out_a.reshape(groups, CAP, ca), plane, split_axis=0, concat_axis=0, tiled=True)
    arrived = arrived.reshape(groups * CAP, ca)
    arrived, payload = lax.optimization_barrier((arrived, payload))
    x_a = lax.all_gather(arrived, "grp", axis=0, tiled=True)

    copies = jnp.broadcast_to(payload[None], (blocks, rows_pad, cb + AUX))
    column = lax.all_to_all(copies, "grp", split_axis=0, concat_axis=0, tiled=True)
    out_b, comb_b = spread_rows(column.reshape(blocks * rows_pad, cb + AUX), top, experts, rows_pad)
    x_b = lax.all_to_all(out_b.reshape(groups, blocks * CAP, cb), plane, split_axis=0, concat_axis=0, tiled=True)
    x_b = x_b.reshape(groups * blocks * CAP, cb)

    w_gate, w_up, w_down, x_a = (
        pltpu.with_memory_space_constraint(w, pltpu.HBM) for w in (w_gate, w_up, w_down, x_a)
    )
    part_up = up_first(x_b, w_gate, w_up, blocks, groups)
    y_a, act = up_rest_down(part_up, x_a, w_gate, w_up, w_down, blocks, groups)
    sum_a = lax.psum_scatter(y_a, "grp", scatter_dimension=0, tiled=True)

    y_b = down(act, w_down, cb, blocks, groups)
    back_b = lax.all_to_all(y_b.reshape(groups, blocks * CAP, cb), plane, split_axis=0, concat_axis=0, tiled=True)
    mixed_b = dot(comb_b, back_b.reshape(groups * blocks * CAP, cb))
    mixed_b = (mixed_b[: blocks * rows_pad] + mixed_b[blocks * rows_pad :]).astype(bf16)
    mixed_b = mixed_b.reshape(blocks, rows_pad, cb)
    mixed_b = lax.all_to_all(mixed_b, "grp", split_axis=0, concat_axis=0, tiled=True)
    routed_b = jnp.sum(mixed_b.astype(f32), axis=0)[:rows_dev]

    sum_a, routed_b = lax.optimization_barrier((sum_a, routed_b))
    back_a = lax.all_to_all(sum_a.reshape(groups, CAP, ca), plane, split_axis=0, concat_axis=0, tiled=True)
    routed_a = dot(comb_a.astype(bf16), back_a.reshape(groups * CAP, ca))
    routed_a = routed_a[:rows_dev] + routed_a[rows_pad : rows_pad + rows_dev]
    routed = jnp.concatenate([routed_a, routed_b], axis=1)
    return (hidden[:rows_dev].astype(f32) + routed).astype(bf16)


def solution(mesh):
    in_specs = (
        P("grp", "role", "dp"),
        P(("role", "grp", "dp"), None),
        P(),
        P(),
        P(("role", "grp", "dp"), None),
        P(("role", "dp"), None, "grp"),
        P(("role", "dp"), None, "grp"),
        P(("role", "dp"), "grp", None),
    )
    out_specs = P(("role", "grp", "dp"), None)
    return jax.shard_map(local, mesh=mesh, in_specs=in_specs, out_specs=out_specs, check_vma=False)
```

time: 301 us -> 229 us (0.76)
  waiting for transfers between devices: 190 us -> 23.6 us
  blocking collectives: 44.3 us -> 151 us
  matrix products: 24.7 us -> 0.71 us
  Pallas kernels: 0 us -> 16 us
    all_to_all x2 -> x6, blocking collectives: 44.3 us -> 151 us  [the longest x1 40.5 us: local(): lax.all_to_all(out_b.reshape(groups, blocks * CAP, cb), plane, split_axis...]
    reduce_scatter x1, waiting for transfers between devices: 83.8 us -> 0.02 us  [local(): sum_a = lax.psum_scatter(y_a, 'grp', scatter_dimension=0, tiled=True)]
    all_gather x1, waiting for transfers between devices: 77.9 us -> 0.02 us  [local(): x_a = lax.all_gather(arrived, 'grp', axis=0, tiled=True)]
    dot_general x5 -> x2, matrix products: 24.7 us -> 0.71 us  [dot(): lax.dot_general(a, b, (contract, ((), ())), preferred_element_type=f32)]
    pallas_call x0 -> x5, Pallas kernels: none -> 16 us  [the longest x1 7.43 us: up_rest_down(): pl.pallas_call(functools.partial(rest_body, blocks, groups), in_specs=[pl...]
    all_to_all x1, waiting for transfers between devices: 28 us -> 23.5 us  [local(): lax.all_to_all(pieces, ('grp', 'dp'), split_axis=0, concat_axis=0, tiled=...]
  transfers between devices with their start and end apart: 3 -> 3, of which waited for: 3 -> 1; matrix products, arithmetic and copies ran while one was open for 0% -> 0% of each run, Pallas kernels for 0% -> 3%
where the time goes in v1:
time: 229 us; the launch traced here: 228 us
  blocking collectives  151 us (66%)
  waiting for transfers between devices  23.6 us (10%)
  starting transfers between devices  16.6 us (7%)
  Pallas kernels  16 us (7%)
  between operations  13.6 us (6%)
  local copies, waits for them, and re-layouts  5.99 us (3%)
    all_to_all x1, blocking collectives, local(): lax.all_to_all(out_b.reshape(groups, blocks * CAP, cb), plane, split_axis...  40.5 us
    all_to_all x1, blocking collectives, local(): lax.all_to_all(y_b.reshape(groups, blocks * CAP, cb), plane, split_axis=0...  37.5 us
    all_to_all x1, waiting for transfers between devices, local(): lax.all_to_all(pieces, ('grp', 'dp'), split_axis=0, concat_axis=0, tiled=...  23.5 us
    all_to_all x1, blocking collectives, local(): lax.all_to_all(sum_a.reshape(groups, CAP, ca), plane, split_axis=0, conca...  19.3 us
    all_to_all x1, blocking collectives, local(): lax.all_to_all(mixed_b, 'grp', split_axis=0, concat_axis=0, tiled=True)  19.2 us
    all_to_all x1, blocking collectives, local(): lax.all_to_all(out_a.reshape(groups, CAP, ca), plane, split_axis=0, conca...  17.9 us
    all_to_all x1, blocking collectives, local(): lax.all_to_all(copies, 'grp', split_axis=0, concat_axis=0, tiled=True)  16.5 us
    all_to_all x1, starting transfers between devices, local(): lax.all_to_all(pieces, ('grp', 'dp'), split_axis=0, concat_axis=0, tiled=...  16.5 us
  transfers between devices with their start and end apart: 3, of which 1 were waited for; matrix products, arithmetic and copies ran while one was open for 0% of the time, Pallas kernels for 3%

profile of v1, /device:TPU:1, one launch (start us, length us, event | category | flops | bytes accessed | tf_op | source)
XLA Modules:
  0.0 228.5 jit_solution(758595857391075682)
XLA Ops:
  6.5 1.4 copy.11
  7.9 0.0 copy-start.2
  7.9 0.0 copy-start.3
  7.9 0.1 pad.12.clone
  8.0 1.4 reshape.43
  9.4 0.0 copy-start.1
  9.4 0.0 copy-start
  9.4 16.5 %all-to-all-start = ((bf16[128,24,128]{2,1,0:T(8,128)(2,1)}), bf16[128,24,128]{2,1,0:T(8,128)(2,1)S(1)}, u32[]{:S(2)}, u32[]{:S(2)}) async-start(bf16[128,24,128]{2,1,0:T(8,128)(2,1)} %reshape.43), calls=%async_computation | async-start | bytes 1572864 | tf_op jit(solution)/shard_map/all_to_all | solution.py:325
  25.9 0.0 all-gather.2.cloned.1.call-start
  25.9 0.0 copy-done.2
  26.0 0.0 copy-done.3
  26.0 23.5 %all-to-all-done = bf16[128,24,128]{2,1,0:T(8,128)(2,1)S(1)} async-done(((bf16[128,24,128]{2,1,0:T(8,128)(2,1)}), bf16[128,24,128]{2,1,0:T(8,128)(2,1)S(1)}, u32[]{:S(2)}, u32[]{:S(2)}) %all-to-all-start) | async-done | bytes 786464 | tf_op jit(solution)/shard_map/all_to_all | solution.py:325
  49.5 0.1 convert_reduce_fusion
  49.6 0.1 copy.10
  49.8 0.1 reshape.45
  49.9 0.0 copy-done.1
  50.0 0.0 copy-done
  50.0 1.0 route.1
  51.0 0.2 reshape.46
  51.2 17.9 %all_to_all.35 = bf16[32,2,4608]{2,1,0:T(2,128)(2,1)S(1)} all-to-all(bf16[32,2,4608]{2,1,0:T(2,128)(2,1)S(1)} %reshape.46), channel_id=1, replica_groups=mesh['role'=2,'grp'=8,'dp'=16] {'role','dp'}, dimensions={0} | all-to-all | bytes 1179648 | tf_op jit(solution)/shard_map/all_to_all | solution.py:336
  69.2 1.0 reshape.47
  70.2 0.0 all-gather.2.cloned.1.call-update
  70.2 0.0 reduce-scatter.2.cloned.1.call-start
  70.3 16.5 %all_to_all.36 = bf16[8,8,2688]{2,1,0:T(8,128)(2,1)S(1)} all-to-all(bf16[8,8,2688]{2,1,0:T(8,128)(2,1)S(1)} %broadcast_in_dim.10), channel_id=1, replica_groups=mesh['role'=2,'grp'=8,'dp'=16] {'grp'}, dimensions={0} | all-to-all | bytes 688128 | tf_op jit(solution)/shard_map/all_to_all | solution.py:342
  86.8 1.3 spread_rows.1
  88.1 40.5 %all_to_all.37 = bf16[32,16,2560]{2,1,0:T(8,128)(2,1)S(1)} all-to-all(bf16[32,16,2560]{2,1,0:T(8,128)(2,1)S(1)} %bitcast.19), channel_id=1, replica_groups=mesh['role'=2,'grp'=8,'dp'=16] {'role','dp'}, dimensions={0} | all-to-all | bytes 5242880 | tf_op jit(solution)/shard_map/all_to_all | solution.py:344
  128.6 3.9 %up_first.1.part_hbm = f32[512,512]{1,0:T(8,128)S(1)} custom-call(bf16[512,2560]{1,0:T(8,128)(2,1)S(1)} %bitcast.18, bf16[1,7168,256]{2,1,0:T(8,128)(2,1)} %wg_hbm.3, bf16[1,7168,256]{2,1,0:T(8,128)(2,1)} %wu_hbm.3), custom_call_target="tpu_custom_call" | custom-call | flops 1342177280 | bytes 5242880 | tf_op jit(solution)/shard_map/up_first/pallas_call | solution.py:203
  132.5 0.0 all-gather.2.cloned.1.call-done.x_hbm
  132.5 7.4 %up_rest_down.1 = (bf16[512,4608]{1,0:T(8,128)(2,1)}, bf16[512,256]{1,0:T(8,128)(2,1)S(1)}) custom-call(f32[512,512]{1,0:T(8,128)S(1)} %up_first.1.part_hbm, bf16[512,4608]{1,0:T(8,128)(2,1)} %all-gather.2.cloned.1.call-done.x_hbm, bf16[1,7168,256]{2,1,0:T(8,128)(2,1)} %wg_hbm.3, bf16[1,7168,256]{2,1,0:T(8,128)(2,1)} %wu_hbm.3, bf16[1,256,7168]{2,1,0:T(8,128)(2,1)} %wd_hbm.3), custom_call_target="tpu_custom_call" | custom-call | flops 3623878656 | bytes 16515072 | tf_op jit(solution)/shard_map/up_rest_down/pallas_call | solution.py:254
  140.0 0.0 reduce-scatter.2.cloned.1.call-update
  140.0 2.4 %down.1 = bf16[512,2560]{1,0:T(8,128)(2,1)S(1)} custom-call(bf16[512,256]{1,0:T(8,128)(2,1)S(1)} %get-tuple-element.24.act_ref, bf16[1,256,7168]{2,1,0:T(8,128)(2,1)} %wd_hbm.3), custom_call_target="tpu_custom_call" | custom-call | flops 671088640 | bytes 3932160 | tf_op jit(solution)/shard_map/down/pallas_call | solution.py:291
  142.4 37.5 %all_to_all.38 = bf16[32,16,2560]{2,1,0:T(8,128)(2,1)S(1)} all-to-all(bf16[32,16,2560]{2,1,0:T(8,128)(2,1)S(1)} %bitcast.17), channel_id=1, replica_groups=mesh['role'=2,'grp'=8,'dp'=16] {'role','dp'}, dimensions={0} | all-to-all | bytes 5242880 | tf_op jit(solution)/shard_map/all_to_all | solution.py:355
  180.0 0.5 fusion.5
  180.5 0.1 fusion.1
  180.6 19.2 %all_to_all.39 = bf16[8,8,2560]{2,1,0:T(8,128)(2,1)S(1)} all-to-all(bf16[8,8,2560]{2,1,0:T(8,128)(2,1)S(1)} %fusion.1), channel_id=1, replica_groups=mesh['role'=2,'grp'=8,'dp'=16] {'grp'}, dimensions={0} | all-to-all | bytes 655360 | tf_op jit(solution)/shard_map/all_to_all | solution.py:359
  199.9 0.0 reduce-scatter.2.cloned.1.call-done
  199.9 1.3 reshape.54
  201.2 19.3 %all_to_all.40 = bf16[32,2,4608]{2,1,0:T(2,128)(2,1)S(1)} all-to-all(bf16[32,2,4608]{2,1,0:T(2,128)(2,1)S(1)} %reshape.54), channel_id=1, replica_groups=mesh['role'=2,'grp'=8,'dp'=16] {'role','dp'}, dimensions={0} | all-to-all | bytes 1179648 | tf_op jit(solution)/shard_map/all_to_all | solution.py:363
  220.5 0.2 reshape.55
  220.7 0.2 fusion.3
  220.9 0.7 fusion.2
  (9 shorter events, 0.2 us)
Async XLA Ops:
  7.9 18.0 %copy-start.2 = (bf16[7168]{0:T(1024)(128)(2,1)S(1)}, bf16[7168]{0:T(1024)(128)(2,1)}, u32[]{:S(2)}) copy-start(bf16[7168]{0:T(1024)(128)(2,1)} %param.10) | copy-start | bytes 43012
  7.9 18.0 %copy-start.3 = (s32[6,8]{1,0:T(8,128)S(1)}, s32[6,8]{1,0:T(8,128)}, u32[]{:S(2)}) copy-start(s32[6,8]{1,0:T(8,128)} %param.12) | copy-start | bytes 580
  9.4 40.5 %copy-start.1 = (bf16[6,7168]{1,0:T(8,128)(2,1)S(1)}, bf16[6,7168]{1,0:T(8,128)(2,1)}, u32[]{:S(2)}) copy-start(bf16[6,7168]{1,0:T(8,128)(2,1)} %param.9) | copy-start | bytes 258052
  9.4 40.6 %copy-start = (bf16[7168,32]{0,1:T(8,128)(2,1)S(1)}, bf16[7168,32]{0,1:T(8,128)(2,1)}, u32[]{:S(2)}) copy-start(bf16[7168,32]{0,1:T(8,128)(2,1)} %param.11) | copy-start | bytes 1376260
  9.4 40.1 %all-to-all-start = ((bf16[128,24,128]{2,1,0:T(8,128)(2,1)}), bf16[128,24,128]{2,1,0:T(8,128)(2,1)S(1)}, u32[]{:S(2)}, u32[]{:S(2)}) async-start(bf16[128,24,128]{2,1,0:T(8,128)(2,1)} %reshape.43), calls=%async_computation | async-start | bytes 1572864 | tf_op jit(solution)/shard_map/all_to_all | solution.py:325
  25.9 106.6 %all-gather.2.cloned.1.call-start = ((), (), s32[]{:S(2)}) async-start(), calls=%async_computation.8 | async-start | bytes 5308416 | tf_op jit(solution)/shard_map/all_gather | solution.py:339
  70.2 129.6 %reduce-scatter.2.cloned.1.call-start = ((), (), s32[]{:S(2)}) async-start(), calls=%async_computation.9 | async-start | bytes 5308416 | tf_op jit(solution)/shard_map/reduce_scatter | solution.py:352
Sparse Core Ops, SparseCore 0:
  70.3 58.6 all-gather.1
  140.1 59.6 reduce-scatter.1

commit v2 on v1

--- a/solution.py
+++ b/solution.py
@@ -8,7 +8,8 @@
 from jax.sharding import PartitionSpec as P
 
 CAP = 2
-B_COLS = 2560
+B_OUT = 2560
+B_BACK = 2688
 UP_CHUNK = 1024
 DOWN_CHUNK = 1024
 VMEM_MIB = 40
@@ -219,15 +220,16 @@
     )(x, w_gate, w_up)
 
 
-def rest_body(blocks, groups, part_hbm, x_hbm, wg_hbm, wu_hbm, wd_hbm, y_hbm, act_ref, *scratch):
+def rest_body(part_hbm, x_hbm, wg_hbm, wu_hbm, wd_hbm, y_hbm, act_ref, *scratch):
     part_buf, x_buf, wg_buf, wu_buf, wd_buf, y_buf, acc, sem, y_sem = scratch
     slots, width = x_hbm.shape
     ff = wg_hbm.shape[2]
     pieces = chunks_of(0, width, UP_CHUNK)
-    downs = chunks_of(0, width, DOWN_CHUNK)
+    back = y_hbm.shape[1]
+    downs = chunks_of(0, back, DOWN_CHUNK)
     wanted = up_loads(pieces, 0, x_hbm, wg_hbm, wu_hbm, x_buf, wg_buf, wu_buf)
     wanted.append((part_hbm, part_buf))
-    wanted.append((wd_hbm.at[0, :, pl.ds(0, width)], wd_buf))
+    wanted.append((wd_hbm.at[0, :, pl.ds(0, back)], wd_buf))
     copies = loads(wanted, sem)
     up_sums(pieces, 0, copies, x_buf, wg_buf, wu_buf, acc)
     copies[-2].wait()
@@ -247,25 +249,25 @@
         copy.wait()
 
 
-def up_rest_down(part, x, w_gate, w_up, w_down, blocks, groups):
+def up_rest_down(part, x, w_gate, w_up, w_down, back):
     slots, width = x.shape
     ff = w_gate.shape[2]
     copies = 3 * len(chunks_of(0, width, UP_CHUNK)) + 2
     return pl.pallas_call(
-        functools.partial(rest_body, blocks, groups),
+        rest_body,
         in_specs=[pl.BlockSpec(memory_space=pl.ANY)] + [pl.BlockSpec(memory_space=pltpu.HBM)] * 4,
         out_specs=[pl.BlockSpec(memory_space=pltpu.HBM), pl.BlockSpec(memory_space=pltpu.VMEM)],
-        out_shape=(pltpu.HBM((slots, width), bf16), jax.ShapeDtypeStruct((slots, ff), bf16)),
+        out_shape=(pltpu.HBM((slots, back), bf16), jax.ShapeDtypeStruct((slots, ff), bf16)),
         scratch_shapes=[
             pltpu.VMEM((slots, 2 * ff), f32),
             pltpu.VMEM((slots, width), bf16),
             pltpu.VMEM((width, ff), bf16),
             pltpu.VMEM((width, ff), bf16),
-            pltpu.VMEM((ff, width), bf16),
-            pltpu.VMEM((slots, width), bf16),
+            pltpu.VMEM((ff, back), bf16),
+            pltpu.VMEM((slots, back), bf16),
             pltpu.VMEM((slots, 2 * ff), f32),
             pltpu.SemaphoreType.DMA((copies,)),
-            pltpu.SemaphoreType.DMA((len(chunks_of(0, width, DOWN_CHUNK)),)),
+            pltpu.SemaphoreType.DMA((len(chunks_of(0, back, DOWN_CHUNK)),)),
         ],
         compiler_params=params(),
         cost_estimate=pl.CostEstimate(
@@ -313,8 +315,8 @@
     rows_dev, width = residual.shape
     experts = router_weight.shape[1]
     top = expert_ids.shape[1]
-    cb = B_COLS
-    ca = width - cb
+    cb, cb_back = B_OUT, B_BACK
+    ca, ca_back = width - cb, width - cb_back
     rows_pad = 8
 
     part = attn_parts[0]
@@ -338,9 +340,10 @@
     arrived, payload = lax.optimization_barrier((arrived, payload))
     x_a = lax.all_gather(arrived, "grp", axis=0, tiled=True)
 
-    copies = jnp.broadcast_to(payload[None], (blocks, rows_pad, cb + AUX))
+    payload = payload[:rows_dev].reshape(-1, 128)
+    copies = jnp.broadcast_to(payload[None], (blocks,) + payload.shape)
     column = lax.all_to_all(copies, "grp", split_axis=0, concat_axis=0, tiled=True)
-    out_b, comb_b = spread_rows(column.reshape(blocks * rows_pad, cb + AUX), top, experts, rows_pad)
+    out_b, comb_b = spread_rows(column.reshape(blocks * rows_dev, cb + AUX), top, experts, rows_dev)
     x_b = lax.all_to_all(out_b.reshape(groups, blocks * CAP, cb), plane, split_axis=0, concat_axis=0, tiled=True)
     x_b = x_b.reshape(groups * blocks * CAP, cb)
 
@@ -348,20 +351,20 @@
         pltpu.with_memory_space_constraint(w, pltpu.HBM) for w in (w_gate, w_up, w_down, x_a)
     )
     part_up = up_first(x_b, w_gate, w_up, blocks, groups)
-    y_a, act = up_rest_down(part_up, x_a, w_gate, w_up, w_down, blocks, groups)
+    y_a, act = up_rest_down(part_up, x_a, w_gate, w_up, w_down, ca_back)
     sum_a = lax.psum_scatter(y_a, "grp", scatter_dimension=0, tiled=True)
 
-    y_b = down(act, w_down, cb, blocks, groups)
-    back_b = lax.all_to_all(y_b.reshape(groups, blocks * CAP, cb), plane, split_axis=0, concat_axis=0, tiled=True)
-    mixed_b = dot(comb_b, back_b.reshape(groups * blocks * CAP, cb))
-    mixed_b = (mixed_b[: blocks * rows_pad] + mixed_b[blocks * rows_pad :]).astype(bf16)
-    mixed_b = mixed_b.reshape(blocks, rows_pad, cb)
+    y_b = down(act, w_down, cb_back, blocks, groups)
+    back_b = lax.all_to_all(y_b.reshape(groups, blocks * CAP, cb_back), plane, split_axis=0, concat_axis=0, tiled=True)
+    mixed_b = dot(comb_b, back_b.reshape(groups * blocks * CAP, cb_back))
+    mixed_b = (mixed_b[: blocks * rows_dev] + mixed_b[blocks * rows_dev :]).astype(bf16)
+    mixed_b = mixed_b.reshape(blocks, -1, 128)
     mixed_b = lax.all_to_all(mixed_b, "grp", split_axis=0, concat_axis=0, tiled=True)
-    routed_b = jnp.sum(mixed_b.astype(f32), axis=0)[:rows_dev]
+    routed_b = jnp.sum(mixed_b.astype(f32), axis=0).reshape(rows_dev, cb_back)
 
     sum_a, routed_b = lax.optimization_barrier((sum_a, routed_b))
-    back_a = lax.all_to_all(sum_a.reshape(groups, CAP, ca), plane, split_axis=0, concat_axis=0, tiled=True)
-    routed_a = dot(comb_a.astype(bf16), back_a.reshape(groups * CAP, ca))
+    back_a = lax.all_to_all(sum_a.reshape(groups, CAP, ca_back), plane, split_axis=0, concat_axis=0, tiled=True)
+    routed_a = dot(comb_a.astype(bf16), back_a.reshape(groups * CAP, ca_back))
     routed_a = routed_a[:rows_dev] + routed_a[rows_pad : rows_pad + rows_dev]
     routed = jnp.concatenate([routed_a, routed_b], axis=1)
     return (hidden[:rows_dev].astype(f32) + routed).astype(bf16)

time: 229 us -> 224 us (0.978)
  blocking collectives: 151 us -> 145 us
    all_to_all x1, blocking collectives: 19.2 us -> 16 us  [local(): lax.all_to_all(mixed_b, 'grp', split_axis=0, concat_axis=0, tiled=True)]
    all_to_all x1, blocking collectives: 16.5 us -> 13.9 us  [local(): lax.all_to_all(copies, 'grp', split_axis=0, concat_axis=0, tiled=True)]
  transfers between devices with their start and end apart: 3 -> 3, of which waited for: 1 -> 1; matrix products, arithmetic and copies ran while one was open for 0% -> 1% of each run, Pallas kernels for 3% -> 3%
where the time goes in v2:
time: 224 us; the launch traced here: 223 us
  blocking collectives  145 us (65%)
  waiting for transfers between devices  23.6 us (11%)
  starting transfers between devices  16.6 us (7%)
  Pallas kernels  16.1 us (7%)
  between operations  13.6 us (6%)
  local copies, waits for them, and re-layouts  6.74 us (3%)
    all_to_all x1, blocking collectives, local(): lax.all_to_all(out_b.reshape(groups, blocks * CAP, cb), plane, split_axis...  40.5 us
    all_to_all x1, blocking collectives, local(): lax.all_to_all(y_b.reshape(groups, blocks * CAP, cb_back), plane, split_a...  38.7 us
    all_to_all x1, waiting for transfers between devices, local(): lax.all_to_all(pieces, ('grp', 'dp'), split_axis=0, concat_axis=0, tiled=...  23.5 us
    all_to_all x1, blocking collectives, local(): lax.all_to_all(out_a.reshape(groups, CAP, ca), plane, split_axis=0, conca...  17.9 us
    all_to_all x1, blocking collectives, local(): lax.all_to_all(sum_a.reshape(groups, CAP, ca_back), plane, split_axis=0,...  17.8 us
    all_to_all x1, starting transfers between devices, local(): lax.all_to_all(pieces, ('grp', 'dp'), split_axis=0, concat_axis=0, tiled=...  16.5 us
    all_to_all x1, blocking collectives, local(): lax.all_to_all(mixed_b, 'grp', split_axis=0, concat_axis=0, tiled=True)  16 us
    all_to_all x1, blocking collectives, local(): lax.all_to_all(copies, 'grp', split_axis=0, concat_axis=0, tiled=True)  13.9 us
  transfers between devices with their start and end apart: 3, of which 1 were waited for; matrix products, arithmetic and copies ran while one was open for 1% of the time, Pallas kernels for 3%

profile of v2, /device:TPU:1, one launch (start us, length us, event | category | flops | bytes accessed | tf_op | source)
XLA Modules:
  0.0 223.1 jit_solution(10828787333423561671)
XLA Ops:
  6.5 0.0 copy-start.2
  6.5 0.0 copy-start.3
  6.5 1.4 copy.11
  7.9 0.1 pad.12.clone
  8.0 0.0 copy-start.1
  8.1 1.4 reshape.46
  9.4 0.0 copy-start
  9.4 16.5 %all-to-all-start = ((bf16[128,24,128]{2,1,0:T(8,128)(2,1)}), bf16[128,24,128]{2,1,0:T(8,128)(2,1)S(1)}, u32[]{:S(2)}, u32[]{:S(2)}) async-start(bf16[128,24,128]{2,1,0:T(8,128)(2,1)} %reshape.46), calls=%async_computation | async-start | bytes 1572864 | tf_op jit(solution)/shard_map/all_to_all | solution.py:327
  25.9 0.0 all-gather.2.cloned.1.call-start
  25.9 0.0 copy-done.2
  26.0 0.0 copy-done.3
  26.0 23.5 %all-to-all-done = bf16[128,24,128]{2,1,0:T(8,128)(2,1)S(1)} async-done(((bf16[128,24,128]{2,1,0:T(8,128)(2,1)}), bf16[128,24,128]{2,1,0:T(8,128)(2,1)S(1)}, u32[]{:S(2)}, u32[]{:S(2)}) %all-to-all-start) | async-done | bytes 786464 | tf_op jit(solution)/shard_map/all_to_all | solution.py:327
  49.5 0.1 convert_reduce_fusion
  49.7 0.1 copy.10
  49.8 0.1 reshape.48
  49.9 0.0 copy-done.1
  50.0 0.0 copy-done
  50.0 1.0 route.1
  51.0 0.2 reshape.49
  51.2 17.9 %all_to_all.35 = bf16[32,2,4608]{2,1,0:T(2,128)(2,1)S(1)} all-to-all(bf16[32,2,4608]{2,1,0:T(2,128)(2,1)S(1)} %reshape.49), channel_id=1, replica_groups=mesh['role'=2,'grp'=8,'dp'=16] {'role','dp'}, dimensions={0} | all-to-all | bytes 1179648 | tf_op jit(solution)/shard_map/all_to_all | solution.py:338
  69.2 1.0 reshape.50
  70.2 0.0 all-gather.2.cloned.1.call-update
  70.2 0.0 reduce-scatter.2.cloned.1.call-start
  70.3 0.1 broadcast_in_dim.11
  70.4 13.9 %all_to_all.36 = bf16[8,126,128]{2,1,0:T(8,128)(2,1)S(1)} all-to-all(bf16[8,126,128]{2,1,0:T(8,128)(2,1)S(1)} %broadcast_in_dim.12), channel_id=1, replica_groups=mesh['role'=2,'grp'=8,'dp'=16] {'grp'}, dimensions={0} | all-to-all | bytes 516096 | tf_op jit(solution)/shard_map/all_to_all | solution.py:345
  84.3 0.3 reshape.51.rows_ref
  84.6 1.2 spread_rows.1
  85.8 40.5 %all_to_all.37 = bf16[32,16,2560]{2,1,0:T(8,128)(2,1)S(1)} all-to-all(bf16[32,16,2560]{2,1,0:T(8,128)(2,1)S(1)} %bitcast.16), channel_id=1, replica_groups=mesh['role'=2,'grp'=8,'dp'=16] {'role','dp'}, dimensions={0} | all-to-all | bytes 5242880 | tf_op jit(solution)/shard_map/all_to_all | solution.py:347
  126.4 3.9 %up_first.1.part_hbm = f32[512,512]{1,0:T(8,128)S(1)} custom-call(bf16[512,2560]{1,0:T(8,128)(2,1)S(1)} %bitcast.15, bf16[1,7168,256]{2,1,0:T(8,128)(2,1)} %wg_hbm.3, bf16[1,7168,256]{2,1,0:T(8,128)(2,1)} %wu_hbm.3), custom_call_target="tpu_custom_call" | custom-call | flops 1342177280 | bytes 5242880 | tf_op jit(solution)/shard_map/up_first/pallas_call | solution.py:204
  130.3 0.0 all-gather.2.cloned.1.call-done.x_hbm
  130.3 7.4 %up_rest_down.1 = (bf16[512,4480]{1,0:T(8,128)(2,1)}, bf16[512,256]{1,0:T(8,128)(2,1)S(1)}) custom-call(f32[512,512]{1,0:T(8,128)S(1)} %up_first.1.part_hbm, bf16[512,4608]{1,0:T(8,128)(2,1)} %all-gather.2.cloned.1.call-done.x_hbm, bf16[1,7168,256]{2,1,0:T(8,128)(2,1)} %wg_hbm.3, bf16[1,7168,256]{2,1,0:T(8,128)(2,1)} %wu_hbm.3, bf16[1,256,7168]{2,1,0:T(8,128)(2,1)} %wd_hbm.3), custom_call_target="tpu_custom_call" | custom-call | flops 3623878656 | bytes 16515072 | tf_op jit(solution)/shard_map/up_rest_down/pallas_call | solution.py:256
  137.7 0.0 reduce-scatter.2.cloned.1.call-update
  137.7 2.6 %down.1 = bf16[512,2688]{1,0:T(8,128)(2,1)S(1)} custom-call(bf16[512,256]{1,0:T(8,128)(2,1)S(1)} %get-tuple-element.24.act_ref, bf16[1,256,7168]{2,1,0:T(8,128)(2,1)} %wd_hbm.3), custom_call_target="tpu_custom_call" | custom-call | flops 704643072 | bytes 4128768 | tf_op jit(solution)/shard_map/down/pallas_call | solution.py:293
  140.3 38.7 %all_to_all.38 = bf16[32,16,2688]{2,1,0:T(8,128)(2,1)S(1)} all-to-all(bf16[32,16,2688]{2,1,0:T(8,128)(2,1)S(1)} %bitcast.14), channel_id=1, replica_groups=mesh['role'=2,'grp'=8,'dp'=16] {'role','dp'}, dimensions={0} | all-to-all | bytes 5505024 | tf_op jit(solution)/shard_map/all_to_all | solution.py:358
  179.0 0.6 fusion.4
  179.6 0.1 fusion
  179.7 0.3 reshape.56
  180.0 16.0 %all_to_all.39 = bf16[8,126,128]{2,1,0:T(8,128)(2,1)S(1)} all-to-all(bf16[8,126,128]{2,1,0:T(8,128)(2,1)S(1)} %reshape.56), channel_id=1, replica_groups=mesh['role'=2,'grp'=8,'dp'=16] {'grp'}, dimensions={0} | all-to-all | bytes 516096 | tf_op jit(solution)/shard_map/all_to_all | solution.py:362
  196.1 0.0 reduce-scatter.2.cloned.1.call-done
  196.1 1.3 reshape.58
  197.4 17.8 %all_to_all.40 = bf16[32,2,4480]{2,1,0:T(2,128)(2,1)S(1)} all-to-all(bf16[32,2,4480]{2,1,0:T(2,128)(2,1)S(1)} %reshape.58), channel_id=1, replica_groups=mesh['role'=2,'grp'=8,'dp'=16] {'role','dp'}, dimensions={0} | all-to-all | bytes 1146880 | tf_op jit(solution)/shard_map/all_to_all | solution.py:366
  215.2 0.2 reshape.59
  215.4 0.2 fusion.2
  215.6 0.7 fusion.1
  (10 shorter events, 0.2 us)
Async XLA Ops:
  6.5 19.4 %copy-start.2 = (bf16[7168]{0:T(1024)(128)(2,1)S(1)}, bf16[7168]{0:T(1024)(128)(2,1)}, u32[]{:S(2)}) copy-start(bf16[7168]{0:T(1024)(128)(2,1)} %param.10) | copy-start | bytes 43012
  6.5 19.4 %copy-start.3 = (s32[6,8]{1,0:T(8,128)S(1)}, s32[6,8]{1,0:T(8,128)}, u32[]{:S(2)}) copy-start(s32[6,8]{1,0:T(8,128)} %param.12) | copy-start | bytes 580
  8.0 41.9 %copy-start.1 = (bf16[6,7168]{1,0:T(8,128)(2,1)S(1)}, bf16[6,7168]{1,0:T(8,128)(2,1)}, u32[]{:S(2)}) copy-start(bf16[6,7168]{1,0:T(8,128)(2,1)} %param.9) | copy-start | bytes 258052
  9.4 40.6 %copy-start = (bf16[7168,32]{0,1:T(8,128)(2,1)S(1)}, bf16[7168,32]{0,1:T(8,128)(2,1)}, u32[]{:S(2)}) copy-start(bf16[7168,32]{0,1:T(8,128)(2,1)} %param.11) | copy-start | bytes 1376260
  9.4 40.1 %all-to-all-start = ((bf16[128,24,128]{2,1,0:T(8,128)(2,1)}), bf16[128,24,128]{2,1,0:T(8,128)(2,1)S(1)}, u32[]{:S(2)}, u32[]{:S(2)}) async-start(bf16[128,24,128]{2,1,0:T(8,128)(2,1)} %reshape.46), calls=%async_computation | async-start | bytes 1572864 | tf_op jit(solution)/shard_map/all_to_all | solution.py:327
  25.9 104.4 %all-gather.2.cloned.1.call-start = ((), (), s32[]{:S(2)}) async-start(), calls=%async_computation.8 | async-start | bytes 5308416 | tf_op jit(solution)/shard_map/all_gather | solution.py:341
  70.2 125.8 %reduce-scatter.2.cloned.1.call-start = ((), (), s32[]{:S(2)}) async-start(), calls=%async_computation.9 | async-start | bytes 5160960 | tf_op jit(solution)/shard_map/reduce_scatter | solution.py:355
Sparse Core Ops, SparseCore 0:
  70.4 56.9 all-gather.1
  137.8 54.6 reduce-scatter.1

commit v3 on v2

--- a/solution.py
+++ b/solution.py
@@ -188,11 +188,28 @@
             acc[:, ff:] += up
 
 
-def up_first_body(blocks, groups, base, x_hbm, wg_hbm, wu_hbm, part_ref, x_buf, wg_buf, wu_buf, acc, sem):
+def up_first_body(blocks, groups, base, x_ref, wg_hbm, wu_hbm, part_ref, wg_buf, wu_buf, acc, sem):
     pieces = chunks_of(base, wg_hbm.shape[1], UP_CHUNK)
-    copies = loads(up_loads(pieces, base, x_hbm, wg_hbm, wu_hbm, x_buf, wg_buf, wu_buf), sem)
+    ff = wg_buf.shape[1]
+    wanted = []
+    for at, size in pieces:
+        here, there = pl.ds(at - base, size), pl.ds(at, size)
+        wanted.append((wg_hbm.at[0, there, :], wg_buf.at[here, :]))
+        wanted.append((wu_hbm.at[0, there, :], wu_buf.at[here, :]))
+    copies = loads(wanted, sem)
     order = reorder(acc.shape[0], blocks, groups, True)
-    up_sums(pieces, base, copies, x_buf, wg_buf, wu_buf, acc)
+    for i, (at, size) in enumerate(pieces):
+        copies[2 * i].wait()
+        copies[2 * i + 1].wait()
+        here = pl.ds(at - base, size)
+        x = x_ref[:, here]
+        gate, up = dot(x, wg_buf[here, :]), dot(x, wu_buf[here, :])
+        if i == 0:
+            acc[:, :ff] = gate
+            acc[:, ff:] = up
+        else:
+            acc[:, :ff] += gate
+            acc[:, ff:] += up
     hi, mid, lo = split3(acc[...])
     part_ref[...] = dot(order, hi) + dot(order, mid) + dot(order, lo)
 
@@ -200,13 +217,12 @@
 def up_first(x, w_gate, w_up, blocks, groups):
     slots, width = x.shape
     _, total, ff = w_gate.shape
-    copies = 3 * len(chunks_of(total - width, total, UP_CHUNK))
+    copies = 2 * len(chunks_of(total - width, total, UP_CHUNK))
     return pl.pallas_call(
         functools.partial(up_first_body, blocks, groups, total - width),
-        in_specs=[pl.BlockSpec(memory_space=pl.ANY)] + [pl.BlockSpec(memory_space=pltpu.HBM)] * 2,
+        in_specs=[pl.BlockSpec(memory_space=pltpu.VMEM)] + [pl.BlockSpec(memory_space=pltpu.HBM)] * 2,
         out_shape=jax.ShapeDtypeStruct((slots, 2 * ff), f32),
         scratch_shapes=[
-            pltpu.VMEM((slots, width), bf16),
             pltpu.VMEM((width, ff), bf16),
             pltpu.VMEM((width, ff), bf16),
             pltpu.VMEM((slots, 2 * ff), f32),

time: 224 us -> 224 us (level)
  no operation moved by 1% of the time
where the time goes in v3:
time: 224 us; the launch traced here: 223 us
  blocking collectives  145 us (65%)
  waiting for transfers between devices  23.6 us (11%)
  starting transfers between devices  16.6 us (7%)
  Pallas kernels  16 us (7%)
  between operations  13.6 us (6%)
  local copies, waits for them, and re-layouts  6.74 us (3%)
    all_to_all x1, blocking collectives, local(): lax.all_to_all(out_b.reshape(groups, blocks * CAP, cb), plane, split_axis...  40.5 us
    all_to_all x1, blocking collectives, local(): lax.all_to_all(y_b.reshape(groups, blocks * CAP, cb_back), plane, split_a...  38.7 us
    all_to_all x1, waiting for transfers between devices, local(): lax.all_to_all(pieces, ('grp', 'dp'), split_axis=0, concat_axis=0, tiled=...  23.5 us
    all_to_all x1, blocking collectives, local(): lax.all_to_all(out_a.reshape(groups, CAP, ca), plane, split_axis=0, conca...  17.9 us
    all_to_all x1, blocking collectives, local(): lax.all_to_all(sum_a.reshape(groups, CAP, ca_back), plane, split_axis=0,...  17.8 us
    all_to_all x1, starting transfers between devices, local(): lax.all_to_all(pieces, ('grp', 'dp'), split_axis=0, concat_axis=0, tiled=...  16.5 us
    all_to_all x1, blocking collectives, local(): lax.all_to_all(mixed_b, 'grp', split_axis=0, concat_axis=0, tiled=True)  16.1 us
    all_to_all x1, blocking collectives, local(): lax.all_to_all(copies, 'grp', split_axis=0, concat_axis=0, tiled=True)  13.9 us
  transfers between devices with their start and end apart: 3, of which 1 were waited for; matrix products, arithmetic and copies ran while one was open for 1% of the time, Pallas kernels for 3%

profile of v3, /device:TPU:1, one launch (start us, length us, event | category | flops | bytes accessed | tf_op | source)
XLA Modules:
  0.0 223.1 jit_solution(13385927352510351106)
XLA Ops:
  6.5 0.0 copy-start.2
  6.5 0.0 copy-start.3
  6.5 1.4 copy.11
  7.9 0.1 pad.12.clone
  8.0 0.0 copy-start.1
  8.1 1.4 reshape.46
  9.4 0.0 copy-start
  9.4 16.5 %all-to-all-start = ((bf16[128,24,128]{2,1,0:T(8,128)(2,1)}), bf16[128,24,128]{2,1,0:T(8,128)(2,1)S(1)}, u32[]{:S(2)}, u32[]{:S(2)}) async-start(bf16[128,24,128]{2,1,0:T(8,128)(2,1)} %reshape.46), calls=%async_computation | async-start | bytes 1572864 | tf_op jit(solution)/shard_map/all_to_all | solution.py:343
  25.9 0.0 all-gather.2.cloned.1.call-start
  25.9 0.0 copy-done.2
  26.0 0.0 copy-done.3
  26.0 23.5 %all-to-all-done = bf16[128,24,128]{2,1,0:T(8,128)(2,1)S(1)} async-done(((bf16[128,24,128]{2,1,0:T(8,128)(2,1)}), bf16[128,24,128]{2,1,0:T(8,128)(2,1)S(1)}, u32[]{:S(2)}, u32[]{:S(2)}) %all-to-all-start) | async-done | bytes 786464 | tf_op jit(solution)/shard_map/all_to_all | solution.py:343
  49.5 0.1 convert_reduce_fusion
  49.7 0.1 copy.10
  49.8 0.1 reshape.48
  49.9 0.0 copy-done.1
  50.0 0.0 copy-done
  50.0 1.0 route.1
  51.0 0.2 reshape.49
  51.2 17.9 %all_to_all.35 = bf16[32,2,4608]{2,1,0:T(2,128)(2,1)S(1)} all-to-all(bf16[32,2,4608]{2,1,0:T(2,128)(2,1)S(1)} %reshape.49), channel_id=1, replica_groups=mesh['role'=2,'grp'=8,'dp'=16] {'role','dp'}, dimensions={0} | all-to-all | bytes 1179648 | tf_op jit(solution)/shard_map/all_to_all | solution.py:354
  69.2 1.0 reshape.50
  70.2 0.0 all-gather.2.cloned.1.call-update
  70.2 0.0 reduce-scatter.2.cloned.1.call-start
  70.3 0.1 broadcast_in_dim.11
  70.4 13.9 %all_to_all.36 = bf16[8,126,128]{2,1,0:T(8,128)(2,1)S(1)} all-to-all(bf16[8,126,128]{2,1,0:T(8,128)(2,1)S(1)} %broadcast_in_dim.12), channel_id=1, replica_groups=mesh['role'=2,'grp'=8,'dp'=16] {'grp'}, dimensions={0} | all-to-all | bytes 516096 | tf_op jit(solution)/shard_map/all_to_all | solution.py:361
  84.3 0.3 reshape.51.rows_ref
  84.6 1.2 spread_rows.1
  85.8 40.5 %all_to_all.37 = bf16[32,16,2560]{2,1,0:T(8,128)(2,1)S(1)} all-to-all(bf16[32,16,2560]{2,1,0:T(8,128)(2,1)S(1)} %bitcast.16), channel_id=1, replica_groups=mesh['role'=2,'grp'=8,'dp'=16] {'role','dp'}, dimensions={0} | all-to-all | bytes 5242880 | tf_op jit(solution)/shard_map/all_to_all | solution.py:363
  126.4 3.8 %up_first.1.part_hbm = f32[512,512]{1,0:T(8,128)S(1)} custom-call(bf16[512,2560]{1,0:T(8,128)(2,1)S(1)} %bitcast.15, bf16[1,7168,256]{2,1,0:T(8,128)(2,1)} %wg_hbm.3, bf16[1,7168,256]{2,1,0:T(8,128)(2,1)} %wu_hbm.3), custom_call_target="tpu_custom_call" | custom-call | flops 1342177280 | bytes 5242880 | tf_op jit(solution)/shard_map/up_first/pallas_call | solution.py:221
  130.2 0.0 all-gather.2.cloned.1.call-done.x_hbm
  130.2 7.4 %up_rest_down.1 = (bf16[512,4480]{1,0:T(8,128)(2,1)}, bf16[512,256]{1,0:T(8,128)(2,1)S(1)}) custom-call(f32[512,512]{1,0:T(8,128)S(1)} %up_first.1.part_hbm, bf16[512,4608]{1,0:T(8,128)(2,1)} %all-gather.2.cloned.1.call-done.x_hbm, bf16[1,7168,256]{2,1,0:T(8,128)(2,1)} %wg_hbm.3, bf16[1,7168,256]{2,1,0:T(8,128)(2,1)} %wu_hbm.3, bf16[1,256,7168]{2,1,0:T(8,128)(2,1)} %wd_hbm.3), custom_call_target="tpu_custom_call" | custom-call | flops 3623878656 | bytes 16515072 | tf_op jit(solution)/shard_map/up_rest_down/pallas_call | solution.py:272
  137.6 0.0 reduce-scatter.2.cloned.1.call-update
  137.6 2.6 %down.1 = bf16[512,2688]{1,0:T(8,128)(2,1)S(1)} custom-call(bf16[512,256]{1,0:T(8,128)(2,1)S(1)} %get-tuple-element.24.act_ref, bf16[1,256,7168]{2,1,0:T(8,128)(2,1)} %wd_hbm.3), custom_call_target="tpu_custom_call" | custom-call | flops 704643072 | bytes 4128768 | tf_op jit(solution)/shard_map/down/pallas_call | solution.py:309
  140.2 38.7 %all_to_all.38 = bf16[32,16,2688]{2,1,0:T(8,128)(2,1)S(1)} all-to-all(bf16[32,16,2688]{2,1,0:T(8,128)(2,1)S(1)} %bitcast.14), channel_id=1, replica_groups=mesh['role'=2,'grp'=8,'dp'=16] {'role','dp'}, dimensions={0} | all-to-all | bytes 5505024 | tf_op jit(solution)/shard_map/all_to_all | solution.py:374
  178.9 0.6 fusion.4
  179.5 0.1 fusion
  179.5 0.3 reshape.56
  179.9 16.1 %all_to_all.39 = bf16[8,126,128]{2,1,0:T(8,128)(2,1)S(1)} all-to-all(bf16[8,126,128]{2,1,0:T(8,128)(2,1)S(1)} %reshape.56), channel_id=1, replica_groups=mesh['role'=2,'grp'=8,'dp'=16] {'grp'}, dimensions={0} | all-to-all | bytes 516096 | tf_op jit(solution)/shard_map/all_to_all | solution.py:378
  196.0 0.0 reduce-scatter.2.cloned.1.call-done
  196.1 1.3 reshape.58
  197.3 17.8 %all_to_all.40 = bf16[32,2,4480]{2,1,0:T(2,128)(2,1)S(1)} all-to-all(bf16[32,2,4480]{2,1,0:T(2,128)(2,1)S(1)} %reshape.58), channel_id=1, replica_groups=mesh['role'=2,'grp'=8,'dp'=16] {'role','dp'}, dimensions={0} | all-to-all | bytes 1146880 | tf_op jit(solution)/shard_map/all_to_all | solution.py:382
  215.2 0.2 reshape.59
  215.4 0.2 fusion.2
  215.6 0.7 fusion.1
  (10 shorter events, 0.2 us)
Async XLA Ops:
  6.5 19.4 %copy-start.2 = (bf16[7168]{0:T(1024)(128)(2,1)S(1)}, bf16[7168]{0:T(1024)(128)(2,1)}, u32[]{:S(2)}) copy-start(bf16[7168]{0:T(1024)(128)(2,1)} %param.10) | copy-start | bytes 43012
  6.5 19.4 %copy-start.3 = (s32[6,8]{1,0:T(8,128)S(1)}, s32[6,8]{1,0:T(8,128)}, u32[]{:S(2)}) copy-start(s32[6,8]{1,0:T(8,128)} %param.12) | copy-start | bytes 580
  8.0 41.9 %copy-start.1 = (bf16[6,7168]{1,0:T(8,128)(2,1)S(1)}, bf16[6,7168]{1,0:T(8,128)(2,1)}, u32[]{:S(2)}) copy-start(bf16[6,7168]{1,0:T(8,128)(2,1)} %param.9) | copy-start | bytes 258052
  9.4 40.6 %copy-start = (bf16[7168,32]{0,1:T(8,128)(2,1)S(1)}, bf16[7168,32]{0,1:T(8,128)(2,1)}, u32[]{:S(2)}) copy-start(bf16[7168,32]{0,1:T(8,128)(2,1)} %param.11) | copy-start | bytes 1376260
  9.4 40.1 %all-to-all-start = ((bf16[128,24,128]{2,1,0:T(8,128)(2,1)}), bf16[128,24,128]{2,1,0:T(8,128)(2,1)S(1)}, u32[]{:S(2)}, u32[]{:S(2)}) async-start(bf16[128,24,128]{2,1,0:T(8,128)(2,1)} %reshape.46), calls=%async_computation | async-start | bytes 1572864 | tf_op jit(solution)/shard_map/all_to_all | solution.py:343
  25.9 104.3 %all-gather.2.cloned.1.call-start = ((), (), s32[]{:S(2)}) async-start(), calls=%async_computation.8 | async-start | bytes 5308416 | tf_op jit(solution)/shard_map/all_gather | solution.py:357
  70.2 125.8 %reduce-scatter.2.cloned.1.call-start = ((), (), s32[]{:S(2)}) async-start(), calls=%async_computation.9 | async-start | bytes 5160960 | tf_op jit(solution)/shard_map/reduce_scatter | solution.py:371
Sparse Core Ops, SparseCore 0:
  70.4 56.9 all-gather.1
  137.7 54.9 reduce-scatter.1

commit v4 on v3

--- a/solution.py
+++ b/solution.py
@@ -337,13 +337,14 @@
 
     part = attn_parts[0]
     col_width = part.shape[1]
-    tiles = -(-col_width // 128)
-    pieces = jnp.pad(part, ((0, 0), (0, tiles * 128 - col_width)))
-    pieces = pieces.reshape(blocks * dp_count, rows_dev * tiles, 128)
+    flat = rows_dev * col_width
+    pairs = -(-flat // 256)
+    pieces = jnp.pad(part.reshape(blocks * dp_count, flat), ((0, 0), (0, pairs * 256 - flat)))
+    pieces = pieces.reshape(blocks * dp_count, pairs, 2, 128)
     received = lax.all_to_all(pieces, ("grp", "dp"), split_axis=0, concat_axis=0, tiled=True)
-    received = received.reshape(blocks, dp_count, rows_dev * tiles, 128)
+    received = received.reshape(blocks, dp_count, pairs, 2, 128)
     attention = jnp.sum(received.astype(f32), axis=0)
-    attention = attention.reshape(dp_count, rows_dev, tiles * 128)[:, :, :col_width]
+    attention = attention.reshape(dp_count, pairs * 256)[:, :flat].reshape(dp_count, rows_dev, col_width)
     attention = attention.transpose(1, 0, 2).reshape(rows_dev, width)
     hidden = (residual.astype(f32) + attention).astype(bf16)
     hidden = jnp.pad(hidden, ((0, rows_pad - rows_dev), (0, 0)))

time: 224 us -> 223 us (level)
  no operation moved by 1% of the time
where the time goes in v4:
time: 223 us
  blocking collectives  145 us (65%)
  waiting for transfers between devices  22.2 us (10%)
  starting transfers between devices  16.6 us (7%)
  Pallas kernels  16 us (7%)
  between operations  13.7 us (6%)
  local copies, waits for them, and re-layouts  7.4 us (3%)
    all_to_all x1, blocking collectives, local(): lax.all_to_all(out_b.reshape(groups, blocks * CAP, cb), plane, split_axis...  40.5 us
    all_to_all x1, blocking collectives, local(): lax.all_to_all(y_b.reshape(groups, blocks * CAP, cb_back), plane, split_a...  38.7 us
    all_to_all x1, waiting for transfers between devices, local(): lax.all_to_all(pieces, ('grp', 'dp'), split_axis=0, concat_axis=0, tiled=...  22.1 us
    all_to_all x1, blocking collectives, local(): lax.all_to_all(out_a.reshape(groups, CAP, ca), plane, split_axis=0, conca...  17.9 us
    all_to_all x1, blocking collectives, local(): lax.all_to_all(sum_a.reshape(groups, CAP, ca_back), plane, split_axis=0,...  17.8 us
    all_to_all x1, starting transfers between devices, local(): lax.all_to_all(pieces, ('grp', 'dp'), split_axis=0, concat_axis=0, tiled=...  16.5 us
    all_to_all x1, blocking collectives, local(): lax.all_to_all(mixed_b, 'grp', split_axis=0, concat_axis=0, tiled=True)  16.1 us
    all_to_all x1, blocking collectives, local(): lax.all_to_all(copies, 'grp', split_axis=0, concat_axis=0, tiled=True)  13.9 us
  transfers between devices with their start and end apart: 3, of which 1 were waited for; matrix products, arithmetic and copies ran while one was open for 1% of the time, Pallas kernels for 3%

profile of v4, /device:TPU:1, one launch (start us, length us, event | category | flops | bytes accessed | tf_op | source)
XLA Modules:
  0.0 223.0 jit_solution(11990208771307669714)
XLA Ops:
  6.5 1.4 copy.9
  7.9 0.0 copy-start.2
  7.9 0.0 copy-start.3
  7.9 0.8 reshape_squeeze.3
  8.8 0.1 pad.12
  8.8 0.0 copy-start.1
  8.8 1.0 reshape.49
  9.9 0.0 copy-start
  9.9 16.5 %all-to-all-start = ((bf16[128,11,2,128]{3,2,1,0:T(2,128)(2,1)}), bf16[128,11,2,128]{3,2,1,0:T(2,128)(2,1)S(1)}, u32[]{:S(2)}, u32[]{:S(2)}) async-start(bf16[128,11,2,128]{3,2,1,0:T(2,128)(2,1)} %reshape.49), calls=%async_computation | async-start | bytes 1441792 | tf_op jit(solution)/shard_map/all_to_all | solution.py:344
  26.3 0.0 all-gather.2.cloned.1.call-start
  26.4 0.0 copy-done.2
  26.4 0.0 copy-done.3
  26.5 22.1 %all-to-all-done = bf16[128,11,2,128]{3,2,1,0:T(2,128)(2,1)S(1)} async-done(((bf16[128,11,2,128]{3,2,1,0:T(2,128)(2,1)}), bf16[128,11,2,128]{3,2,1,0:T(2,128)(2,1)S(1)}, u32[]{:S(2)}, u32[]{:S(2)}) %all-to-all-start) | async-done | bytes 720928 | tf_op jit(solution)/shard_map/all_to_all | solution.py:344
  48.6 0.6 convert_reduce_fusion
  49.2 0.1 reshape.50
  49.4 0.1 reshape.51
  49.5 0.1 copy.10
  49.6 0.1 reshape.52
  49.8 0.0 copy-done.1
  49.9 0.0 copy-done
  49.9 1.0 route.1
  50.9 0.2 reshape.53
  51.1 17.9 %all_to_all.35 = bf16[32,2,4608]{2,1,0:T(2,128)(2,1)S(1)} all-to-all(bf16[32,2,4608]{2,1,0:T(2,128)(2,1)S(1)} %reshape.53), channel_id=1, replica_groups=mesh['role'=2,'grp'=8,'dp'=16] {'role','dp'}, dimensions={0} | all-to-all | bytes 1179648 | tf_op jit(solution)/shard_map/all_to_all | solution.py:355
  69.0 1.0 reshape.54
  70.0 0.0 all-gather.2.cloned.1.call-update
  70.1 0.0 reduce-scatter.2.cloned.1.call-start
  70.1 0.1 broadcast_in_dim.11
  70.2 13.9 %all_to_all.36 = bf16[8,126,128]{2,1,0:T(8,128)(2,1)S(1)} all-to-all(bf16[8,126,128]{2,1,0:T(8,128)(2,1)S(1)} %broadcast_in_dim.12), channel_id=1, replica_groups=mesh['role'=2,'grp'=8,'dp'=16] {'grp'}, dimensions={0} | all-to-all | bytes 516096 | tf_op jit(solution)/shard_map/all_to_all | solution.py:362
  84.1 0.3 reshape.55.rows_ref
  84.4 1.2 spread_rows.1
  85.7 40.5 %all_to_all.37 = bf16[32,16,2560]{2,1,0:T(8,128)(2,1)S(1)} all-to-all(bf16[32,16,2560]{2,1,0:T(8,128)(2,1)S(1)} %bitcast.14), channel_id=1, replica_groups=mesh['role'=2,'grp'=8,'dp'=16] {'role','dp'}, dimensions={0} | all-to-all | bytes 5242880 | tf_op jit(solution)/shard_map/all_to_all | solution.py:364
  126.2 3.8 %up_first.1.part_hbm = f32[512,512]{1,0:T(8,128)S(1)} custom-call(bf16[512,2560]{1,0:T(8,128)(2,1)S(1)} %bitcast.13, bf16[1,7168,256]{2,1,0:T(8,128)(2,1)} %wg_hbm.3, bf16[1,7168,256]{2,1,0:T(8,128)(2,1)} %wu_hbm.3), custom_call_target="tpu_custom_call" | custom-call | flops 1342177280 | bytes 5242880 | tf_op jit(solution)/shard_map/up_first/pallas_call | solution.py:221
  130.0 0.0 all-gather.2.cloned.1.call-done.x_hbm
  130.0 7.4 %up_rest_down.1 = (bf16[512,4480]{1,0:T(8,128)(2,1)}, bf16[512,256]{1,0:T(8,128)(2,1)S(1)}) custom-call(f32[512,512]{1,0:T(8,128)S(1)} %up_first.1.part_hbm, bf16[512,4608]{1,0:T(8,128)(2,1)} %all-gather.2.cloned.1.call-done.x_hbm, bf16[1,7168,256]{2,1,0:T(8,128)(2,1)} %wg_hbm.3, bf16[1,7168,256]{2,1,0:T(8,128)(2,1)} %wu_hbm.3, bf16[1,256,7168]{2,1,0:T(8,128)(2,1)} %wd_hbm.3), custom_call_target="tpu_custom_call" | custom-call | flops 3623878656 | bytes 16515072 | tf_op jit(solution)/shard_map/up_rest_down/pallas_call | solution.py:272
  137.4 0.0 reduce-scatter.2.cloned.1.call-update
  137.4 2.6 %down.1 = bf16[512,2688]{1,0:T(8,128)(2,1)S(1)} custom-call(bf16[512,256]{1,0:T(8,128)(2,1)S(1)} %get-tuple-element.24.act_ref, bf16[1,256,7168]{2,1,0:T(8,128)(2,1)} %wd_hbm.3), custom_call_target="tpu_custom_call" | custom-call | flops 704643072 | bytes 4128768 | tf_op jit(solution)/shard_map/down/pallas_call | solution.py:309
  140.0 38.7 %all_to_all.38 = bf16[32,16,2688]{2,1,0:T(8,128)(2,1)S(1)} all-to-all(bf16[32,16,2688]{2,1,0:T(8,128)(2,1)S(1)} %bitcast.12), channel_id=1, replica_groups=mesh['role'=2,'grp'=8,'dp'=16] {'role','dp'}, dimensions={0} | all-to-all | bytes 5505024 | tf_op jit(solution)/shard_map/all_to_all | solution.py:375
  178.7 0.6 fusion.4
  179.3 0.1 fusion
  179.4 0.3 reshape.60
  179.7 16.1 %all_to_all.39 = bf16[8,126,128]{2,1,0:T(8,128)(2,1)S(1)} all-to-all(bf16[8,126,128]{2,1,0:T(8,128)(2,1)S(1)} %reshape.60), channel_id=1, replica_groups=mesh['role'=2,'grp'=8,'dp'=16] {'grp'}, dimensions={0} | all-to-all | bytes 516096 | tf_op jit(solution)/shard_map/all_to_all | solution.py:379
  195.9 0.0 reduce-scatter.2.cloned.1.call-done
  195.9 1.3 reshape.62
  197.2 17.8 %all_to_all.40 = bf16[32,2,4480]{2,1,0:T(2,128)(2,1)S(1)} all-to-all(bf16[32,2,4480]{2,1,0:T(2,128)(2,1)S(1)} %reshape.62), channel_id=1, replica_groups=mesh['role'=2,'grp'=8,'dp'=16] {'role','dp'}, dimensions={0} | all-to-all | bytes 1146880 | tf_op jit(solution)/shard_map/all_to_all | solution.py:383
  215.0 0.2 reshape.63
  215.2 0.2 fusion.2
  215.4 0.7 fusion.1
  (9 shorter events, 0.2 us)
Async XLA Ops:
  7.9 18.5 %copy-start.2 = (bf16[7168]{0:T(1024)(128)(2,1)S(1)}, bf16[7168]{0:T(1024)(128)(2,1)}, u32[]{:S(2)}) copy-start(bf16[7168]{0:T(1024)(128)(2,1)} %param.10) | copy-start | bytes 43012
  7.9 18.5 %copy-start.3 = (s32[6,8]{1,0:T(8,128)S(1)}, s32[6,8]{1,0:T(8,128)}, u32[]{:S(2)}) copy-start(s32[6,8]{1,0:T(8,128)} %param.12) | copy-start | bytes 580
  8.8 41.0 %copy-start.1 = (bf16[6,7168]{1,0:T(8,128)(2,1)S(1)}, bf16[6,7168]{1,0:T(8,128)(2,1)}, u32[]{:S(2)}) copy-start(bf16[6,7168]{1,0:T(8,128)(2,1)} %param.9) | copy-start | bytes 258052
  9.9 40.0 %copy-start = (bf16[7168,32]{0,1:T(8,128)(2,1)S(1)}, bf16[7168,32]{0,1:T(8,128)(2,1)}, u32[]{:S(2)}) copy-start(bf16[7168,32]{0,1:T(8,128)(2,1)} %param.11) | copy-start | bytes 1376260
  9.9 38.7 %all-to-all-start = ((bf16[128,11,2,128]{3,2,1,0:T(2,128)(2,1)}), bf16[128,11,2,128]{3,2,1,0:T(2,128)(2,1)S(1)}, u32[]{:S(2)}, u32[]{:S(2)}) async-start(bf16[128,11,2,128]{3,2,1,0:T(2,128)(2,1)} %reshape.49), calls=%async_computation | async-start | bytes 1441792 | tf_op jit(solution)/shard_map/all_to_all | solution.py:344
  26.3 103.7 %all-gather.2.cloned.1.call-start = ((), (), s32[]{:S(2)}) async-start(), calls=%async_computation.8 | async-start | bytes 5308416 | tf_op jit(solution)/shard_map/all_gather | solution.py:358
  70.1 125.8 %reduce-scatter.2.cloned.1.call-start = ((), (), s32[]{:S(2)}) async-start(), calls=%async_computation.9 | async-start | bytes 5160960 | tf_op jit(solution)/shard_map/reduce_scatter | solution.py:372
Sparse Core Ops, SparseCore 0:
  70.2 56.9 all-gather.1
  137.6 54.8 reduce-scatter.1
